TPU v7x, 512 devices: a whole 4x8x8 slice. The times are simulated.
512 devices in a mesh: seq: 256 (over x, y, z), batch: 2 (over core).
Axes of the slice: x: 4, y: 8, z: 8, core: 2. Of those that a mesh axis runs over, the one named last changes fastest.
Arguments:
- query_in: bfloat16 [262144, 1024], P(('batch', 'seq')), parts along dimension 0, may hold values from -6 to 6
- key_in: bfloat16 [262144, 1024], P(('batch', 'seq')), parts along dimension 0, may hold values from -6 to 6
- value_in: bfloat16 [262144, 1024], P(('batch', 'seq')), parts along dimension 0, may hold values from -6 to 6
- conv_weight: float32 [3, 4, 1024], replicated, may hold values from -3 to 3
- level_weights: float32 [5, 8, 262144], P(None, None, ('batch', 'seq')), parts along dimension 2, may hold values from 0.1 to 1
- out_gain: float32 [1024], replicated, may hold values from 0.25 to 1.75
Outputs:
- mixed_out: bfloat16 [262144, 1024], P(('batch', 'seq')), parts along dimension 0
There are 2 independent parts, one for each index of `batch`. A program takes and returns all parts, laid end to end along the dimension named above; an argument that names none is the same for every part. Nothing has to cross between parts.
All inputs are finite; a program needn't handle non-finite values.
Results may differ from a plain program's by a relative error of at most 0.005.
Values may be sent and summed in bfloat16 or wider, within the bound.
A program may use at most 64 MiB of HBM per device.

v0:
```python
import jax
import jax.numpy as jnp
from jax import lax
from jax.sharding import PartitionSpec as P

LEVELS = 4


EPS = 1e-06


def shifted(array, axis, by):
    size = lax.axis_size(axis)
    pairs = [(i, i + by) for i in range(size) if 0 <= i + by < size]
    return lax.ppermute(array, axis, pairs)


def from_partner(value, axis, bit):
    mask = 2**bit
    pairs = [(source, source ^ mask) for source in range(lax.axis_size(axis))]
    return lax.ppermute(value, axis, pairs)


def short_conv(stream, rim_rows, kernel):
    values = stream.astype(jnp.float32)
    tap_count = kernel.shape[0]
    padded = jnp.concatenate([rim_rows.astype(jnp.float32), values], axis=0)
    summed = jnp.zeros_like(values)
    for offset in range(tap_count):
        summed = summed + kernel[offset] * padded[offset : offset + values.shape[0]]
    return jax.nn.silu(summed)


def unit_heads(values, head_count, head_size):
    shaped = values.reshape(values.shape[0], head_count, head_size)
    return (shaped / jnp.sqrt(jnp.sum(shaped * shaped, axis=-1, keepdims=True) + EPS)).astype(
        jnp.bfloat16
    )


def shards(query_in, key_in, value_in, conv_weight, level_weights, out_gain):
    rows_here = query_in.shape[0]
    width = query_in.shape[1]
    head_count = level_weights.shape[1]
    head_size = width // head_count
    tap_count = conv_weight.shape[1]
    edge = rows_here - tap_count + 1
    rim_query, rim_key, rim_value = shifted(
        (query_in[edge:], key_in[edge:], value_in[edge:]), "seq", 1
    )
    queries = unit_heads(short_conv(query_in, rim_query, conv_weight[0]), head_count, head_size)
    keys = unit_heads(short_conv(key_in, rim_key, conv_weight[1]), head_count, head_size)
    values = (
        short_conv(value_in, rim_value, conv_weight[2])
        .reshape(rows_here, head_count, head_size)
        .astype(jnp.bfloat16)
    )
    span_state = jnp.einsum("chd,che->hde", keys, values, preferred_element_type=jnp.float32)
    device_count = lax.axis_size("seq")
    bit_total = device_count.bit_length() - 1
    per_level = bit_total // LEVELS
    branching = 2**per_level
    index_here = lax.axis_index("seq")
    buckets = [jnp.zeros_like(span_state) for level_index in range(LEVELS)]
    running = span_state
    for bit_index in range(bit_total):
        partner = from_partner(running.astype(jnp.bfloat16), "seq", bit_index).astype(running.dtype)
        upper_half = (jnp.right_shift(index_here, bit_index) % 2).astype(jnp.float32)
        level_index = bit_index // per_level
        buckets[level_index] = buckets[level_index] + upper_half * partner
        if bit_index + 1 < bit_total:
            running = running + partner
    positions = jnp.arange(rows_here)
    scores = jnp.einsum("thd,shd->hts", queries, keys, preferred_element_type=jnp.float32)
    causal_mask = (positions[None, :] <= positions[:, None]).astype(jnp.float32)
    weights = (scores * causal_mask / jnp.sqrt(positions + 1.0)[:, None]).astype(jnp.bfloat16)
    local_mix = jnp.einsum("hts,shd->thd", weights, values, preferred_element_type=jnp.float32)
    weights_here = jnp.transpose(level_weights, (0, 2, 1))
    mixed = weights_here[0][:, :, None] * local_mix
    query_wide = queries.astype(jnp.float32)
    for level_index in range(LEVELS):
        child = branching**level_index
        parent = branching ** (level_index + 1)
        tokens_before = rows_here * (index_here % parent - index_here % child)
        level_scale = 1.0 / jnp.sqrt(jnp.maximum(tokens_before, 1).astype(jnp.float32))
        projected = jnp.einsum(
            "thd,hde->the", query_wide, buckets[level_index], precision=lax.Precision.HIGHEST
        )
        mixed = mixed + (weights_here[level_index + 1] * level_scale)[:, :, None] * projected
    normed = (
        mixed
        / jnp.sqrt(jnp.mean(mixed * mixed, axis=-1, keepdims=True) + EPS)
        * out_gain.reshape(head_count, head_size)
    )
    return normed.astype(jnp.bfloat16).reshape(rows_here, width)


def solution(mesh):
    return jax.shard_map(
        shards,
        mesh=mesh,
        in_specs=(
            P(("batch", "seq"), None),
            P(("batch", "seq"), None),
            P(("batch", "seq"), None),
            P(),
            P(None, None, ("batch", "seq")),
            P(),
        ),
        out_specs=P(("batch", "seq"), None),
        check_vma=False,
    )
```

profile of v0, /device:TPU:92, one launch (start us, length us, event | category | flops | bytes accessed | tf_op | source)
XLA Modules:
  0.0 138.4 jit_solution(5812197859589885978)
XLA Ops:
  0.0 0.8 slice.116
  0.8 4.3 %collective-permute-start = (bf16[3,1024]{1,0:T(4,128)(2,1)S(1)}, bf16[3,1024]{1,0:T(4,128)(2,1)S(1)}, u32[]{:S(2)}, u32[]{:S(2)}) collective-permute-start(bf16[3,1024]{1,0:T(4,128)(2,1)S(1)} %slice.116), channel_id=1, source_target_pairs={{0,2},{2,4},{4,6},{6,8},{8,10},{10,12},{12,14},{14,16},{16,18},{18... | collective-permute-start | bytes 18440 | tf_op jit(solution)/shard_map/ppermute | solution.py:15
  5.1 0.7 slice.132
  5.8 4.3 %collective-permute-start.2 = (bf16[3,1024]{1,0:T(4,128)(2,1)S(1)}, bf16[3,1024]{1,0:T(4,128)(2,1)S(1)}, u32[]{:S(2)}, u32[]{:S(2)}) collective-permute-start(bf16[3,1024]{1,0:T(4,128)(2,1)S(1)} %slice.132), channel_id=1, source_target_pairs={{0,2},{2,4},{4,6},{6,8},{8,10},{10,12},{12,14},{14,16},{16,18},{18... | collective-permute-start | bytes 18440 | tf_op jit(solution)/shard_map/ppermute | solution.py:15
  10.1 0.7 slice.124
  10.8 5.5 %collective-permute-start.1 = (bf16[3,1024]{1,0:T(4,128)(2,1)S(1)}, bf16[3,1024]{1,0:T(4,128)(2,1)S(1)}, u32[]{:S(2)}, u32[]{:S(2)}) collective-permute-start(bf16[3,1024]{1,0:T(4,128)(2,1)S(1)} %slice.124), channel_id=1, source_target_pairs={{0,2},{2,4},{4,6},{6,8},{8,10},{10,12},{12,14},{14,16},{16,18},{18... | collective-permute-start | bytes 18440 | tf_op jit(solution)/shard_map/ppermute | solution.py:15
  16.3 1.0 fusion.76
  17.4 1.5 %convert_element_type.143 = f32[512,1024]{1,0:T(8,128)S(1)} convert(bf16[512,1024]{1,0:T(8,128)(2,1)} %param.7) | non-fusion elementwise | flops 524288 | bytes 3145728 | tf_op jit(solution)/shard_map/convert_element_type | solution.py:25
  18.8 1.6 %convert_element_type.136 = f32[512,1024]{1,0:T(8,128)} convert(bf16[512,1024]{1,0:T(8,128)(2,1)S(1)} %copy-done.13) | non-fusion elementwise | flops 524288 | bytes 3145728 | tf_op jit(solution)/shard_map/convert_element_type | solution.py:25
  20.6 1.3 multiply_bitcast_fusion
  22.4 0.6 multiply_reduce_fusion.1
  23.3 0.9 divide_convert_fusion.2
  24.2 1.5 %copy.54 = bf16[512,8,128]{0,2,1:T(8,128)(2,1)} copy(bf16[512,8,128]{2,1,0:T(8,128)(2,1)S(1)} %divide_convert_fusion.2) | data formatting | bytes 2097152 | tf_op jit(solution)/shard_map/convert_element_type | solution.py:36
  26.1 1.3 fusion.35
  28.0 0.5 copy-done.3
  28.5 1.9 %collective-permute-start.3 = (bf16[8,128,128]{2,1,0:T(8,128)(2,1)S(1)}, bf16[8,128,128]{2,1,0:T(8,128)(2,1)S(1)}, u32[]{:S(2)}, u32[]{:S(2)}) collective-permute-start(bf16[8,128,128]{2,1,0:T(8,128)(2,1)S(1)} %get-tuple-element.24), channel_id=1, source_target_pairs={{0,2},{2,0},{4,6},{6,4},{8,10},{10,8},{12,14},{14,12},{16,18},{18,... | collective-permute-start | bytes 786440 | tf_op jit(solution)/shard_map/ppermute | solution.py:21
  30.4 1.1 fusion.34
  31.5 1.5 %convert_element_type.140 = f32[512,1024]{1,0:T(8,128)S(1)} convert(bf16[512,1024]{1,0:T(8,128)(2,1)} %param.6) | non-fusion elementwise | flops 524288 | bytes 3145728 | tf_op jit(solution)/shard_map/convert_element_type | solution.py:25
  33.1 4.5 %collective-permute-done.3 = bf16[8,128,128]{2,1,0:T(8,128)(2,1)S(1)} collective-permute-done((bf16[8,128,128]{2,1,0:T(8,128)(2,1)S(1)}, bf16[8,128,128]{2,1,0:T(8,128)(2,1)S(1)}, u32[]{:S(2)}, u32[]{:S(2)}) %collective-permute-start.3) | collective-permute-done | bytes 262176 | tf_op jit(solution)/shard_map/ppermute | solution.py:21
  37.6 4.3 %collective-permute-start.4 = (bf16[8,128,128]{2,1,0:T(8,128)(2,1)S(1)}, bf16[8,128,128]{2,1,0:T(8,128)(2,1)S(1)}, u32[]{:S(2)}, u32[]{:S(2)}) collective-permute-start(bf16[8,128,128]{2,1,0:T(8,128)(2,1)S(1)} %fusion.58), channel_id=1, source_target_pairs={{0,4},{2,6},{4,0},{6,2},{8,12},{10,14},{12,8},{14,10},{16,20},{18,... | collective-permute-start | bytes 786440 | tf_op jit(solution)/shard_map/ppermute | solution.py:21
  41.9 1.3 multiply_bitcast_fusion.1
  43.7 7.6 %collective-permute-done.4 = bf16[8,128,128]{2,1,0:T(8,128)(2,1)S(1)} collective-permute-done((bf16[8,128,128]{2,1,0:T(8,128)(2,1)S(1)}, bf16[8,128,128]{2,1,0:T(8,128)(2,1)S(1)}, u32[]{:S(2)}, u32[]{:S(2)}) %collective-permute-start.4) | collective-permute-done | bytes 262176 | tf_op jit(solution)/shard_map/ppermute | solution.py:21
  51.3 0.7 copy-done.5
  52.0 0.8 fusion.74
  52.8 3.2 %collective-permute-start.5 = (bf16[8,128,128]{2,1,0:T(8,128)(2,1)}, bf16[8,128,128]{2,1,0:T(8,128)(2,1)S(1)}, u32[]{:S(2)}, u32[]{:S(2)}) collective-permute-start(bf16[8,128,128]{2,1,0:T(8,128)(2,1)} %fusion.74), channel_id=1, source_target_pairs={{0,8},{2,10},{4,12},{6,14},{8,0},{10,2},{12,4},{14,6},{16,24},{18,... | collective-permute-start | bytes 786440 | tf_op jit(solution)/shard_map/ppermute | solution.py:21
  56.1 1.3 multiply_reduce_fusion.2
  57.4 1.0 copy.47
  58.5 0.8 copy.48
  59.3 10.4 %collective-permute-done.5 = bf16[8,128,128]{2,1,0:T(8,128)(2,1)S(1)} collective-permute-done((bf16[8,128,128]{2,1,0:T(8,128)(2,1)}, bf16[8,128,128]{2,1,0:T(8,128)(2,1)S(1)}, u32[]{:S(2)}, u32[]{:S(2)}) %collective-permute-start.5) | collective-permute-done | bytes 262176 | tf_op jit(solution)/shard_map/ppermute | solution.py:21
  69.8 0.6 copy-done.9
  70.4 2.3 %collective-permute-start.6 = (bf16[8,128,128]{2,1,0:T(8,128)(2,1)S(1)}, bf16[8,128,128]{2,1,0:T(8,128)(2,1)S(1)}, u32[]{:S(2)}, u32[]{:S(2)}) collective-permute-start(bf16[8,128,128]{2,1,0:T(8,128)(2,1)S(1)} %fusion.59), channel_id=1, source_target_pairs={{0,16},{2,18},{4,20},{6,22},{8,24},{10,26},{12,28},{14,30},{16,0},... | collective-permute-start | bytes 786440 | tf_op jit(solution)/shard_map/ppermute | solution.py:21
  72.7 1.7 %divide_convert_fusion.3 = bf16[512,8,128]{2,1,0:T(8,128)(2,1)S(1)} fusion(f32[512,8]{1,0:T(8,128)} %copy.48, f32[64,8,8,128]{3,2,1,0:T(8,128)S(1)} %copy.70), kind=kLoop, calls=%fused_computation.50 | loop fusion | flops 1048576 | bytes 3162112 | tf_op jit(solution)/shard_map/convert_element_type | solution.py:36
  74.4 5.2 %collective-permute-done.6 = bf16[8,128,128]{2,1,0:T(8,128)(2,1)S(1)} collective-permute-done((bf16[8,128,128]{2,1,0:T(8,128)(2,1)S(1)}, bf16[8,128,128]{2,1,0:T(8,128)(2,1)S(1)}, u32[]{:S(2)}, u32[]{:S(2)}) %collective-permute-start.6) | collective-permute-done | bytes 262176 | tf_op jit(solution)/shard_map/ppermute | solution.py:21
  79.8 0.5 copy-done.14
  80.3 2.2 %collective-permute-start.7 = (bf16[8,128,128]{2,1,0:T(8,128)(2,1)S(1)}, bf16[8,128,128]{2,1,0:T(8,128)(2,1)S(1)}, u32[]{:S(2)}, u32[]{:S(2)}) collective-permute-start(bf16[8,128,128]{2,1,0:T(8,128)(2,1)S(1)} %get-tuple-element.5), channel_id=1, source_target_pairs={{0,32},{2,34},{4,36},{6,38},{8,40},{10,42},{12,44},{14,46},{16,48}... | collective-permute-start | bytes 786440 | tf_op jit(solution)/shard_map/ppermute | solution.py:21
  82.5 5.8 %fusion = f32[8,128,512]{2,1,0:T(8,128)} fusion(f32[512]{0:T(512)S(1)} %add_sqrt_fusion.3, f32[512,512]{1,0:T(8,128)} %fusion.34, bf16[512,8,128]{0,2,1:T(8,128)(2,1)} %copy.54, bf16[64,8,8,128]{3,2,1,0:T(8,128)(2,1)} %copy-done.3, bf16[512,8,128]{2,1,0:T(8,128)(2,1)S(1)} %divide_convert_fusion.3), kind=kOutput, calls=%fused_computation.1 | convolution fusion | flops 1080033280 | bytes 6293504 | tf_op jit(solution)/shard_map/hts,shd->thd/dot_general | solution.py:77
  88.3 6.6 %collective-permute-done.7 = bf16[8,128,128]{2,1,0:T(8,128)(2,1)S(1)} collective-permute-done((bf16[8,128,128]{2,1,0:T(8,128)(2,1)S(1)}, bf16[8,128,128]{2,1,0:T(8,128)(2,1)S(1)}, u32[]{:S(2)}, u32[]{:S(2)}) %collective-permute-start.7) | collective-permute-done | bytes 262176 | tf_op jit(solution)/shard_map/ppermute | solution.py:21
  94.9 5.2 %collective-permute-start.8 = (bf16[8,128,128]{2,1,0:T(8,128)(2,1)S(1)}, bf16[8,128,128]{2,1,0:T(8,128)(2,1)S(1)}, u32[]{:S(2)}, u32[]{:S(2)}) collective-permute-start(bf16[8,128,128]{2,1,0:T(8,128)(2,1)S(1)} %fusion.60), channel_id=1, source_target_pairs={{0,64},{2,66},{4,68},{6,70},{8,72},{10,74},{12,76},{14,78},{16,80}... | collective-permute-start | bytes 786440 | tf_op jit(solution)/shard_map/ppermute | solution.py:21
  100.2 1.1 fusion.43
  101.3 12.4 %collective-permute-done.8 = bf16[8,128,128]{2,1,0:T(8,128)(2,1)S(1)} collective-permute-done((bf16[8,128,128]{2,1,0:T(8,128)(2,1)S(1)}, bf16[8,128,128]{2,1,0:T(8,128)(2,1)S(1)}, u32[]{:S(2)}, u32[]{:S(2)}) %collective-permute-start.8) | collective-permute-done | bytes 262176 | tf_op jit(solution)/shard_map/ppermute | solution.py:21
  113.8 3.3 %collective-permute-start.9 = (bf16[8,128,128]{2,1,0:T(8,128)(2,1)S(1)}, bf16[8,128,128]{2,1,0:T(8,128)(2,1)S(1)}, u32[]{:S(2)}, u32[]{:S(2)}) collective-permute-start(bf16[8,128,128]{2,1,0:T(8,128)(2,1)S(1)} %fusion.69), channel_id=1, source_target_pairs={{0,128},{2,130},{4,132},{6,134},{8,136},{10,138},{12,140},{14,142}... | collective-permute-start | bytes 786440 | tf_op jit(solution)/shard_map/ppermute | solution.py:21
  117.1 1.1 fusion.41
  118.2 5.7 %collective-permute-done.9 = bf16[8,128,128]{2,1,0:T(8,128)(2,1)S(1)} collective-permute-done((bf16[8,128,128]{2,1,0:T(8,128)(2,1)S(1)}, bf16[8,128,128]{2,1,0:T(8,128)(2,1)S(1)}, u32[]{:S(2)}, u32[]{:S(2)}) %collective-permute-start.9) | collective-permute-done | bytes 262176 | tf_op jit(solution)/shard_map/ppermute | solution.py:21
  124.0 2.5 %collective-permute-start.10 = (bf16[8,128,128]{2,1,0:T(8,128)(2,1)S(1)}, bf16[8,128,128]{2,1,0:T(8,128)(2,1)S(1)}, u32[]{:S(2)}, u32[]{:S(2)}) collective-permute-start(bf16[8,128,128]{2,1,0:T(8,128)(2,1)S(1)} %fusion.55), channel_id=1, source_target_pairs={{0,256},{2,258},{4,260},{6,262},{8,264},{10,266},{12,268},{14,270}... | collective-permute-start | bytes 786440 | tf_op jit(solution)/shard_map/ppermute | solution.py:21
  126.6 1.1 fusion.39
  127.7 7.3 %collective-permute-done.10 = bf16[8,128,128]{2,1,0:T(8,128)(2,1)S(1)} collective-permute-done((bf16[8,128,128]{2,1,0:T(8,128)(2,1)S(1)}, bf16[8,128,128]{2,1,0:T(8,128)(2,1)S(1)}, u32[]{:S(2)}, u32[]{:S(2)}) %collective-permute-start.10) | collective-permute-done | bytes 262176 | tf_op jit(solution)/shard_map/ppermute | solution.py:21
  135.0 1.8 %multiply_reduce_fusion = (f32[512,8]{0,1:T(8,128)S(1)}, f32[512,8,128]{0,2,1:T(8,128)S(1)}) fusion(bf16[512,8,128]{2,1,0:T(8,128)(2,1)S(1)} %divide_convert_fusion.3, bf16[8,128,128]{2,1,0:T(8,128)(2,1)S(1)} %collective-permute-done.9, bf16[8,128,128]{2,1,0:T(8,128)(2,1)S(1)} %collective-permute-done.10, f32[]{:T(128)S(6)} %convert_element_type.173, ...), kind=kOutput, calls=%fused_computation.46 | convolution fusion | flops 811724800 | bytes 12156936 | tf_op jit(solution)/shard_map/thd,hde->the/dot_general | solution.py:86
  137.0 1.3 copy.64
  (55 shorter events, 3.2 us)
Async XLA Ops:
  0.0 18.8 %copy-start.13 = (bf16[512,1024]{1,0:T(8,128)(2,1)S(1)}, bf16[512,1024]{1,0:T(8,128)(2,1)}, u32[]{:S(2)}) copy-start(bf16[512,1024]{1,0:T(8,128)(2,1)} %param.8) | copy-start | bytes 3145732
  0.8 24.8 %collective-permute-start = (bf16[3,1024]{1,0:T(4,128)(2,1)S(1)}, bf16[3,1024]{1,0:T(4,128)(2,1)S(1)}, u32[]{:S(2)}, u32[]{:S(2)}) collective-permute-start(bf16[3,1024]{1,0:T(4,128)(2,1)S(1)} %slice.116), channel_id=1, source_target_pairs={{0,2},{2,4},{4,6},{6,8},{8,10},{10,12},{12,14},{14,16},{16,18},{18... | collective-permute-start | bytes 18440 | tf_op jit(solution)/shard_map/ppermute | solution.py:15
  5.8 14.8 %collective-permute-start.2 = (bf16[3,1024]{1,0:T(4,128)(2,1)S(1)}, bf16[3,1024]{1,0:T(4,128)(2,1)S(1)}, u32[]{:S(2)}, u32[]{:S(2)}) collective-permute-start(bf16[3,1024]{1,0:T(4,128)(2,1)S(1)} %slice.132), channel_id=1, source_target_pairs={{0,2},{2,4},{4,6},{6,8},{8,10},{10,12},{12,14},{14,16},{16,18},{18... | collective-permute-start | bytes 18440 | tf_op jit(solution)/shard_map/ppermute | solution.py:15
  10.8 22.2 %collective-permute-start.1 = (bf16[3,1024]{1,0:T(4,128)(2,1)S(1)}, bf16[3,1024]{1,0:T(4,128)(2,1)S(1)}, u32[]{:S(2)}, u32[]{:S(2)}) collective-permute-start(bf16[3,1024]{1,0:T(4,128)(2,1)S(1)} %slice.124), channel_id=1, source_target_pairs={{0,2},{2,4},{4,6},{6,8},{8,10},{10,12},{12,14},{14,16},{16,18},{18... | collective-permute-start | bytes 18440 | tf_op jit(solution)/shard_map/ppermute | solution.py:15
  24.2 2.0 %copy-start.2 = (f32[512,1024]{1,0:T(8,128)S(1)}, f32[512,1024]{1,0:T(8,128)}, u32[]{:S(2)}) copy-start(f32[512,1024]{1,0:T(8,128)} %convert_element_type.136) | copy-start | bytes 6291460
  25.6 1.9 %copy-start.4 = (bf16[512,8,128]{0,2,1:T(8,128)(2,1)S(1)}, bf16[512,8,128]{0,2,1:T(8,128)(2,1)}, u32[]{:S(2)}) copy-start(bf16[512,8,128]{0,2,1:T(8,128)(2,1)} %copy.54) | copy-start | bytes 3145732
  27.5 1.0 copy-start.3
  27.5 2.9 %copy-start.16 = (f32[5,8,512]{2,1,0:T(8,128)S(1)}, f32[5,8,512]{2,1,0:T(8,128)}, u32[]{:S(2)}) copy-start(f32[5,8,512]{2,1,0:T(8,128)} %param.10) | copy-start | bytes 245764
  28.5 41.2 %copy-start = (f32[8,128,128]{2,1,0:T(8,128)}, f32[8,128,128]{2,1,0:T(8,128)S(1)}, u32[]{:S(2)}) copy-start(f32[8,128,128]{2,1,0:T(8,128)S(1)} %get-tuple-element.25) | copy-start | bytes 1572868
  28.5 9.1 %collective-permute-start.3 = (bf16[8,128,128]{2,1,0:T(8,128)(2,1)S(1)}, bf16[8,128,128]{2,1,0:T(8,128)(2,1)S(1)}, u32[]{:S(2)}, u32[]{:S(2)}) collective-permute-start(bf16[8,128,128]{2,1,0:T(8,128)(2,1)S(1)} %get-tuple-element.24), channel_id=1, source_target_pairs={{0,2},{2,0},{4,6},{6,4},{8,10},{10,8},{12,14},{14,12},{16,18},{18,... | collective-permute-start | bytes 786440 | tf_op jit(solution)/shard_map/ppermute | solution.py:21
  37.6 13.7 %collective-permute-start.4 = (bf16[8,128,128]{2,1,0:T(8,128)(2,1)S(1)}, bf16[8,128,128]{2,1,0:T(8,128)(2,1)S(1)}, u32[]{:S(2)}, u32[]{:S(2)}) collective-permute-start(bf16[8,128,128]{2,1,0:T(8,128)(2,1)S(1)} %fusion.58), channel_id=1, source_target_pairs={{0,4},{2,6},{4,0},{6,2},{8,12},{10,14},{12,8},{14,10},{16,20},{18,... | collective-permute-start | bytes 786440 | tf_op jit(solution)/shard_map/ppermute | solution.py:21
  51.3 0.7 copy-start.5
  52.8 16.9 %copy-start.6 = (bf16[8,128,128]{2,1,0:T(8,128)(2,1)S(1)}, bf16[8,128,128]{2,1,0:T(8,128)(2,1)}, u32[]{:S(2)}) copy-start(bf16[8,128,128]{2,1,0:T(8,128)(2,1)} %copy-done.5) | copy-start | bytes 786436
  52.8 16.9 %collective-permute-start.5 = (bf16[8,128,128]{2,1,0:T(8,128)(2,1)}, bf16[8,128,128]{2,1,0:T(8,128)(2,1)S(1)}, u32[]{:S(2)}, u32[]{:S(2)}) collective-permute-start(bf16[8,128,128]{2,1,0:T(8,128)(2,1)} %fusion.74), channel_id=1, source_target_pairs={{0,8},{2,10},{4,12},{6,14},{8,0},{10,2},{12,4},{14,6},{16,24},{18,... | collective-permute-start | bytes 786440 | tf_op jit(solution)/shard_map/ppermute | solution.py:21
  69.7 0.7 copy-start.9
  70.4 9.2 %copy-start.1 = (f32[8,128,128]{2,1,0:T(8,128)S(1)}, f32[8,128,128]{2,1,0:T(8,128)}, u32[]{:S(2)}) copy-start(f32[8,128,128]{2,1,0:T(8,128)} %copy-done) | copy-start | bytes 1572868
  70.4 9.2 %copy-start.7 = (bf16[8,128,128]{2,1,0:T(8,128)(2,1)S(1)}, bf16[8,128,128]{2,1,0:T(8,128)(2,1)}, u32[]{:S(2)}) copy-start(bf16[8,128,128]{2,1,0:T(8,128)(2,1)} %copy-done.5) | copy-start | bytes 786436
  70.4 9.2 %collective-permute-start.6 = (bf16[8,128,128]{2,1,0:T(8,128)(2,1)S(1)}, bf16[8,128,128]{2,1,0:T(8,128)(2,1)S(1)}, u32[]{:S(2)}, u32[]{:S(2)}) collective-permute-start(bf16[8,128,128]{2,1,0:T(8,128)(2,1)S(1)} %fusion.59), channel_id=1, source_target_pairs={{0,16},{2,18},{4,20},{6,22},{8,24},{10,26},{12,28},{14,30},{16,0},... | collective-permute-start | bytes 786440 | tf_op jit(solution)/shard_map/ppermute | solution.py:21
  72.7 6.9 %copy-start.10 = (bf16[8,128,128]{2,1,0:T(8,128)(2,1)S(1)}, bf16[8,128,128]{2,1,0:T(8,128)(2,1)}, u32[]{:S(2)}) copy-start(bf16[8,128,128]{2,1,0:T(8,128)(2,1)} %copy-done.9) | copy-start | bytes 786436
  79.6 0.7 copy-start.14
  80.3 19.9 %copy-start.8 = (bf16[8,128,128]{2,1,0:T(8,128)(2,1)S(1)}, bf16[8,128,128]{2,1,0:T(8,128)(2,1)}, u32[]{:S(2)}) copy-start(bf16[8,128,128]{2,1,0:T(8,128)(2,1)} %copy-done.5) | copy-start | bytes 786436
  80.3 14.6 %collective-permute-start.7 = (bf16[8,128,128]{2,1,0:T(8,128)(2,1)S(1)}, bf16[8,128,128]{2,1,0:T(8,128)(2,1)S(1)}, u32[]{:S(2)}, u32[]{:S(2)}) collective-permute-start(bf16[8,128,128]{2,1,0:T(8,128)(2,1)S(1)} %get-tuple-element.5), channel_id=1, source_target_pairs={{0,32},{2,34},{4,36},{6,38},{8,40},{10,42},{12,44},{14,46},{16,48}... | collective-permute-start | bytes 786440 | tf_op jit(solution)/shard_map/ppermute | solution.py:21
  94.9 22.1 %copy-start.11 = (bf16[8,128,128]{2,1,0:T(8,128)(2,1)S(1)}, bf16[8,128,128]{2,1,0:T(8,128)(2,1)}, u32[]{:S(2)}) copy-start(bf16[8,128,128]{2,1,0:T(8,128)(2,1)} %copy-done.9) | copy-start | bytes 786436
  94.9 22.1 %copy-start.15 = (bf16[8,128,128]{2,1,0:T(8,128)(2,1)S(1)}, bf16[8,128,128]{2,1,0:T(8,128)(2,1)}, u32[]{:S(2)}) copy-start(bf16[8,128,128]{2,1,0:T(8,128)(2,1)} %copy-done.14) | copy-start | bytes 786436
  94.9 18.7 %collective-permute-start.8 = (bf16[8,128,128]{2,1,0:T(8,128)(2,1)S(1)}, bf16[8,128,128]{2,1,0:T(8,128)(2,1)S(1)}, u32[]{:S(2)}, u32[]{:S(2)}) collective-permute-start(bf16[8,128,128]{2,1,0:T(8,128)(2,1)S(1)} %fusion.60), channel_id=1, source_target_pairs={{0,64},{2,66},{4,68},{6,70},{8,72},{10,74},{12,76},{14,78},{16,80}... | collective-permute-start | bytes 786440 | tf_op jit(solution)/shard_map/ppermute | solution.py:21
  113.8 10.1 %collective-permute-start.9 = (bf16[8,128,128]{2,1,0:T(8,128)(2,1)S(1)}, bf16[8,128,128]{2,1,0:T(8,128)(2,1)S(1)}, u32[]{:S(2)}, u32[]{:S(2)}) collective-permute-start(bf16[8,128,128]{2,1,0:T(8,128)(2,1)S(1)} %fusion.69), channel_id=1, source_target_pairs={{0,128},{2,130},{4,132},{6,134},{8,136},{10,138},{12,140},{14,142}... | collective-permute-start | bytes 786440 | tf_op jit(solution)/shard_map/ppermute | solution.py:21
  124.0 10.9 %copy-start.12 = (f32[8,128,512]{2,1,0:T(8,128)S(1)}, f32[8,128,512]{2,1,0:T(8,128)}, u32[]{:S(2)}) copy-start(f32[8,128,512]{2,1,0:T(8,128)} %fusion) | copy-start | bytes 6291460
  124.0 10.9 %collective-permute-start.10 = (bf16[8,128,128]{2,1,0:T(8,128)(2,1)S(1)}, bf16[8,128,128]{2,1,0:T(8,128)(2,1)S(1)}, u32[]{:S(2)}, u32[]{:S(2)}) collective-permute-start(bf16[8,128,128]{2,1,0:T(8,128)(2,1)S(1)} %fusion.55), channel_id=1, source_target_pairs={{0,256},{2,258},{4,260},{6,262},{8,264},{10,266},{12,268},{14,270}... | collective-permute-start | bytes 786440 | tf_op jit(solution)/shard_map/ppermute | solution.py:21
  135.0 1.8 %copy-start.17 = (f32[1024]{0:T(1024)S(1)}, f32[1024]{0:T(1024)}, u32[]{:S(2)}) copy-start(f32[1024]{0:T(1024)} %param.11) | copy-start | bytes 12292
where the time goes:
time: 139 us; the launch traced here: 138 us
  waiting for transfers between devices  59.6 us (43%)
  starting transfers between devices  39 us (28%)
  other arithmetic  15.8 us (11%)
  local copies, waits for them, and re-layouts  11.9 us (9%)
  matrix products  11.3 us (8%)
    ppermute x8, waiting for transfers between devices, from_partner(): return lax.ppermute(value, axis, pairs)  59.6 us
    ppermute x8, starting transfers between devices, from_partner(): return lax.ppermute(value, axis, pairs)  25 us
    ppermute x3, starting transfers between devices, shifted(): return lax.ppermute(array, axis, pairs)  14 us
    dot_general x1, matrix products, shards(): jnp.einsum('hts,shd->thd', weights, values, preferred_element_type=jnp.fl...  5.79 us
    dot_general x4, matrix products, shards(): jnp.einsum('thd,hde->the', query_wide, buckets[level_index], precision=la...  5.01 us
    convert_element_type x3, other arithmetic, short_conv(): values = stream.astype(jnp.float32)  4.5 us
    unnamed x3, other arithmetic  3.96 us
    unnamed x38, local copies, waits for them, and re-layouts  3.79 us
  transfers between devices with their start and end apart: 11, of which 8 were waited for; matrix products, arithmetic and copies ran while one was open for 22% of the time, Pallas kernels for 0%

commit v1 on v0

v1 whole, which is shorter than its diff:
```python
import functools

import jax
import jax.numpy as jnp
from jax import lax
from jax.experimental import pallas as pl
from jax.experimental.pallas import tpu as pltpu
from jax.sharding import PartitionSpec as P

MESH = pl.DeviceIdType.MESH
EPS = 1e-6
H = 8
DK = 128
T = 512
NX, NY, NZ = 4, 8, 8
F32 = jnp.float32
BF16 = jnp.bfloat16


def level_factor(digit, level):
    base = (1.0 / (T * 4.0**level)) ** 0.5
    return jnp.where(
        digit == 0, 0.0, jnp.where(digit == 1, base, jnp.where(digit == 2, base * 0.5**0.5, base * (1.0 / 3.0) ** 0.5))
    )


def kernel(
    q_hbm, k_hbm, v_hbm, cw_ref, lw_ref, gain_ref, out_hbm,
    xin, tails, halo_f, halo_send, halo_recv, xf, xfs, qs, ks, vs, lwh, acc,
    state, a_recv, b0_send, b1_send, yr, xt, buckets, obuf, own_f,
    in_sem, tail_sem, out_sem, halo_sem, a_ss, a_rs, y_ss, y_rs, x_ss, x_rs, b_ss, b_rs,
):
    me = lax.axis_index("seq")
    core = lax.axis_index("batch")
    x, y, z = me // 64, lax.rem(me // 8, 8), lax.rem(me, 8)

    def dev(xx, yy, zz):
        return (xx * 64 + yy * 8 + zz, core)

    ins = (q_hbm, k_hbm, v_hbm)

    def head_of(step):
        return lax.rem(z + 1 + step, NZ)

    def load(stream, head):
        cols = pl.ds(pl.multiple_of(head * DK, DK), DK)
        return pltpu.make_async_copy(ins[stream].at[:, cols], xin.at[stream, head], in_sem.at[stream, head])

    def tail(stream):
        return pltpu.make_async_copy(ins[stream].at[pl.ds(T - 16, 16), :], tails.at[stream], tail_sem.at[stream])

    for stream in range(3):
        tail(stream).start()

    def start_loads(step, carry):
        for stream in (1, 2):
            load(stream, head_of(step)).start()
        return carry

    lax.fori_loop(0, H, start_loads, 0)

    def start_q(head, carry):
        load(0, head).start()
        return carry

    lax.fori_loop(0, H, start_q, 0)

    barrier = pltpu.get_barrier_semaphore()

    def greet_ring(step, carry):
        pl.semaphore_signal(barrier, inc=1, device_id=dev(x, y, lax.rem(z + step, NZ)), device_id_type=MESH)
        pl.semaphore_signal(barrier, inc=1, device_id=dev(x, lax.rem(y + step, NY), z), device_id_type=MESH)
        return carry

    lax.fori_loop(1, NZ, greet_ring, 0)
    for step in range(1, NX):
        pl.semaphore_signal(barrier, inc=1, device_id=dev(lax.rem(x + step, NX), y, z), device_id_type=MESH)
    pl.semaphore_signal(barrier, inc=1, device_id=(lax.rem(me + 255, 256), core), device_id_type=MESH)

    halo_f[...] = jnp.zeros_like(halo_f)
    for stream in range(3):
        tail(stream).wait()
        halo_f[pl.ds(3 * stream, 3), :] = tails[stream].astype(F32)[13:16, :]
    halo_send[...] = halo_f[...].astype(BF16)
    halo = pltpu.make_async_remote_copy(
        halo_send, halo_recv, halo_sem.at[0], halo_sem.at[1], device_id=(lax.rem(me + 1, 256), core), device_id_type=MESH
    )

    pl.semaphore_wait(barrier, 18)
    halo.start()

    lw = jnp.concatenate([lw_ref[...], jnp.zeros((128 - 5 * H, T), F32)], axis=0).T
    pos = lax.broadcasted_iota(jnp.int32, (T, 128), 0).astype(F32)
    lane = lax.broadcasted_iota(jnp.int32, (T, 128), 1)
    lw = jnp.where(lane < H, lw * lax.rsqrt(pos + 1.0), lw)
    for head in range(H):
        lwh[head] = lw if head == 0 else pltpu.roll(lw, 128 - head, 1)

    ones = jnp.ones((DK, DK), BF16)

    def taps(stream, head):
        cols = pl.ds(pl.multiple_of(head * DK, DK), DK)
        return [cw_ref[stream, pl.ds(j, 1), cols] for j in range(4)]

    def silu(c):
        return c * pl.reciprocal(1.0 + jnp.exp(-c), approx=True)

    def unit(a):
        total = jnp.dot((a * a).astype(BF16), ones, preferred_element_type=F32)
        return a * lax.rsqrt(total + EPS)

    def conv_rows(src, w, row, count):
        c = w[0] * src[pl.ds(row + 5, count), :]
        for j in range(1, 4):
            c = c + w[j] * src[pl.ds(row + 5 + j, count), :]
        return silu(c)

    CH = 128

    def stream_head(stream, head, dst, halo_rows):
        w = taps(stream, head)
        buf = xf.at[stream]
        if halo_rows is None:
            buf[pl.ds(0, 8), :] = jnp.zeros((8, DK), F32)
        else:
            buf[pl.ds(5, 3), :] = halo_rows
        buf[pl.ds(8, T), :] = xin[stream, head].astype(F32)
        for row in range(0, T, CH):
            a = conv_rows(buf, w, row, CH)
            if stream < 2:
                a = unit(a)
            dst[head, pl.ds(row, CH), :] = a.astype(BF16)

    def kv_step(step, carry):
        head = head_of(step)
        for stream, dst in ((1, ks), (2, vs)):
            load(stream, head).wait()
            stream_head(stream, head, dst, None)
        return carry

    lax.fori_loop(0, H, kv_step, 0)

    halo.wait()
    halo_f[...] = jnp.where(me == 0, 0.0, halo_recv[...].astype(F32))

    def halo_rows(stream, head):
        cols = pl.ds(pl.multiple_of(head * DK, DK), DK)
        return halo_f[pl.ds(3 * stream, 3), cols]

    def to_owner(head):
        return pltpu.make_async_remote_copy(
            state.at[head], a_recv.at[z], a_ss.at[head], a_rs.at[z], device_id=dev(x, y, head), device_id_type=MESH
        )

    def from_row(source):
        return pltpu.make_async_remote_copy(
            state.at[source], a_recv.at[source], a_ss.at[source], a_rs.at[source],
            device_id=dev(x, y, source), device_id_type=MESH,
        )

    def state_of(head):
        for stream, dst in ((1, ks), (2, vs)):
            xfs[pl.ds(5, 3), :] = halo_rows(stream, head)
            xfs[pl.ds(8, 16), :] = xin[stream, head, pl.ds(0, 16), :].astype(F32)
            a = conv_rows(xfs, taps(stream, head), 0, 16)
            if stream == 1:
                a = unit(a)
            dst[head, pl.ds(0, 16), :] = a.astype(BF16)
        return lax.dot_general(ks[head], vs[head], (((0,), (0,)), ((), ())), preferred_element_type=F32)

    def state_step(step, carry):
        head = head_of(step)
        state[head] = state_of(head).astype(BF16)
        to_owner(head).start()
        return carry

    lax.fori_loop(0, H - 1, state_step, 0)
    a_recv[z] = state_of(z).astype(BF16)

    row_i = lax.broadcasted_iota(jnp.int32, (256, 256), 0)
    col_i = lax.broadcasted_iota(jnp.int32, (256, 256), 1)
    causal = row_i >= col_i
    NT = (((1,), (1,)), ((), ()))

    def weight(head, level):
        return jnp.broadcast_to(lwh[head, :, pl.ds(8 * level, 1)], (T, DK))

    def local_step(head, carry):
        load(0, head).wait()
        stream_head(0, head, qs, halo_rows(0, head))
        q0, q1 = qs[head, pl.ds(0, 256), :], qs[head, pl.ds(256, 256), :]
        k0, k1 = ks[head, pl.ds(0, 256), :], ks[head, pl.ds(256, 256), :]
        v0, v1 = vs[head, pl.ds(0, 256), :], vs[head, pl.ds(256, 256), :]
        s00 = jnp.where(causal, lax.dot_general(q0, k0, NT, preferred_element_type=F32), 0.0).astype(BF16)
        s10 = lax.dot_general(q1, k0, NT, preferred_element_type=F32).astype(BF16)
        s11 = jnp.where(causal, lax.dot_general(q1, k1, NT, preferred_element_type=F32), 0.0).astype(BF16)
        o0 = jnp.dot(s00, v0, preferred_element_type=F32)
        o1 = jnp.dot(s10, v0, preferred_element_type=F32) + jnp.dot(s11, v1, preferred_element_type=F32)
        w = weight(head, 0)
        acc[head, pl.ds(0, 256), :] = w[:256] * o0
        acc[head, pl.ds(256, 256), :] = w[256:] * o1
        return carry

    lax.fori_loop(0, H, local_step, 0)

    def wait_row(step, carry):
        from_row(lax.rem(z + step, NZ)).wait_recv()
        return carry

    lax.fori_loop(1, NZ, wait_row, 0)
    own_lo = None
    row_sum = None
    for zz in range(NZ):
        s = a_recv[zz].astype(F32)
        if zz % 4 == 0:
            b0_send[zz] = jnp.zeros((DK, DK), BF16)
            group = s
        else:
            b0_send[zz] = (group * ((1.0 / (T * (zz % 4))) ** 0.5)).astype(BF16)
            group = group + s
        if zz == 3:
            own_lo = group
        if zz == 7:
            row_sum = own_lo + group
    own_f[0] = own_lo
    yr[y] = row_sum.astype(BF16)

    def row_copy(src_y, dst_y, sem_y):
        return pltpu.make_async_remote_copy(
            yr.at[src_y], yr.at[src_y], y_ss.at[dst_y], y_rs.at[src_y], device_id=dev(x, dst_y, z), device_id_type=MESH
        )

    def send_rows(step, carry):
        to = lax.rem(y + step, NY)
        row_copy(y, to, y).start()
        return carry

    lax.fori_loop(1, NY, send_rows, 0)

    def bucket_copy(level, src, to, head):
        return pltpu.make_async_remote_copy(
            src, buckets.at[level, head], b_ss.at[level, to], b_rs.at[level, head], device_id=dev(x, y, to), device_id_type=MESH
        )

    def send_b0(step, carry):
        to = lax.rem(z + step, NZ)
        bucket_copy(0, b0_send.at[to], to, z).start()
        return carry

    lax.fori_loop(1, NZ, send_b0, 0)
    buckets[0, z] = b0_send[z]

    def wait_rows(step, carry):
        src = lax.rem(y + step, NY)
        row_copy(src, src, src).wait_recv()
        return carry

    lax.fori_loop(1, NY, wait_rows, 0)

    odd = lax.rem(y, 2)
    pair = y // 2
    before = jnp.where(odd == 1, 1.0, 0.0) * yr[jnp.maximum(y - 1, 0)].astype(F32)
    b1_send[0] = (level_factor(2 * odd, 1) * before).astype(BF16)
    b1_send[1] = (level_factor(2 * odd + 1, 1) * (before + own_f[0])).astype(BF16)
    earlier = jnp.zeros((DK, DK), F32)
    plane = jnp.zeros((DK, DK), F32)
    for yy in range(NY):
        r = yr[yy].astype(F32)
        plane = plane + r
        earlier = earlier + jnp.where(yy < 2 * pair, 1.0, 0.0) * r
    b1_send[2] = (level_factor(pair, 2) * earlier).astype(BF16)
    xt[x] = plane.astype(BF16)

    def plane_copy(src_x, dst_x):
        return pltpu.make_async_remote_copy(
            xt.at[src_x], xt.at[src_x], x_ss.at[dst_x], x_rs.at[src_x], device_id=dev(dst_x, y, z), device_id_type=MESH
        )

    for step in range(1, NX):
        plane_copy(x, lax.rem(x + step, NX)).start()

    def send_b12(step, carry):
        to = lax.rem(z + step, NZ)
        bucket_copy(1, b1_send.at[to // 4], to, z).start()
        return carry

    lax.fori_loop(1, NZ, send_b12, 0)

    def send_b2(step, carry):
        to = lax.rem(z + step, NZ)
        bucket_copy(2, b1_send.at[2], to, z).start()
        return carry

    lax.fori_loop(1, NZ, send_b2, 0)
    buckets[1, z] = b1_send[z // 4]
    buckets[2, z] = b1_send[2]

    def wait_bucket(level, head):
        @pl.when(head != z)
        def _():
            bucket_copy(level, b1_send.at[2], head, head).wait_recv()

    def project(level, head):
        return weight(head, level + 1) * jnp.dot(qs[head], buckets[level, head], preferred_element_type=F32)

    def add_level(level):
        def step(i, carry):
            head = lax.rem(z + i, NZ)
            wait_bucket(level, head)
            acc[head] += project(level, head)
            return carry

        lax.fori_loop(0, H, step, 0)

    for step in range(1, NX):
        src = lax.rem(x + step, NX)
        plane_copy(src, src).wait_recv()
    earlier = jnp.zeros((DK, DK), F32)
    for xx in range(NX):
        earlier = earlier + jnp.where(xx < x, 1.0, 0.0) * xt[xx].astype(F32)
    b1_send[3] = (level_factor(x, 3) * earlier).astype(BF16)

    def send_b3(step, carry):
        to = lax.rem(z + step, NZ)
        bucket_copy(3, b1_send.at[3], to, z).start()
        return carry

    lax.fori_loop(1, NZ, send_b3, 0)
    buckets[3, z] = b1_send[3]

    add_level(0)
    add_level(1)
    add_level(2)

    def store(head):
        cols = pl.ds(pl.multiple_of(head * DK, DK), DK)
        return pltpu.make_async_copy(obuf.at[head], out_hbm.at[:, cols], out_sem.at[head])

    def last_step(i, carry):
        head = lax.rem(z + i, NZ)
        wait_bucket(3, head)
        mixed = acc[head] + project(3, head)
        total = jnp.dot((mixed * mixed).astype(BF16), ones, preferred_element_type=F32)
        cols = pl.ds(pl.multiple_of(head * DK, DK), DK)
        obuf[head] = (mixed * lax.rsqrt(total * (1.0 / DK) + EPS) * gain_ref[:, cols]).astype(BF16)
        store(head).start()
        return carry

    lax.fori_loop(0, H, last_step, 0)

    def drain(step, carry):
        to = lax.rem(z + step, NZ)
        from_row(to).wait_send()
        ty = lax.rem(y + step, NY)
        row_copy(y, ty, y).wait_send()
        for level in range(4):
            bucket_copy(level, b1_send.at[2], to, z).wait_send()
        return carry

    lax.fori_loop(1, NZ, drain, 0)
    for step in range(1, NX):
        plane_copy(x, lax.rem(x + step, NX)).wait_send()

    def stored(head, carry):
        store(head).wait()
        return carry

    lax.fori_loop(0, H, stored, 0)


def shards(query_in, key_in, value_in, conv_weight, level_weights, out_gain):
    anywhere = pl.BlockSpec(memory_space=pl.ANY)
    vmem = pl.BlockSpec(memory_space=pltpu.VMEM)
    dma = pltpu.SemaphoreType.DMA
    return pl.pallas_call(
        kernel,
        out_shape=jax.ShapeDtypeStruct((T, H * DK), BF16),
        in_specs=[anywhere] * 3 + [vmem] * 3,
        out_specs=anywhere,
        scratch_shapes=[
            pltpu.VMEM((3, H, T, DK), BF16),
            pltpu.VMEM((3, 16, H * DK), BF16),
            pltpu.VMEM((16, H * DK), F32),
            pltpu.VMEM((16, H * DK), BF16),
            pltpu.VMEM((16, H * DK), BF16),
            pltpu.VMEM((3, T + 8, DK), F32),
            pltpu.VMEM((24, DK), F32),
            pltpu.VMEM((H, T, DK), BF16),
            pltpu.VMEM((H, T, DK), BF16),
            pltpu.VMEM((H, T, DK), BF16),
            pltpu.VMEM((H, T, DK), F32),
            pltpu.VMEM((H, T, DK), F32),
            pltpu.VMEM((H, DK, DK), BF16),
            pltpu.VMEM((NZ, DK, DK), BF16),
            pltpu.VMEM((NZ, DK, DK), BF16),
            pltpu.VMEM((4, DK, DK), BF16),
            pltpu.VMEM((NY, DK, DK), BF16),
            pltpu.VMEM((NX, DK, DK), BF16),
            pltpu.VMEM((4, H, DK, DK), BF16),
            pltpu.VMEM((H, T, DK), BF16),
            pltpu.VMEM((1, DK, DK), F32),
            dma((3, H)),
            dma((3,)),
            dma((H,)),
            dma((2,)),
            dma((NZ,)),
            dma((NZ,)),
            dma((NY,)),
            dma((NY,)),
            dma((NX,)),
            dma((NX,)),
            dma((4, NZ)),
            dma((4, NZ)),
        ],
        compiler_params=pltpu.CompilerParams(
            collective_id=0, has_side_effects=True, vmem_limit_bytes=48 * 1024 * 1024
        ),
        cost_estimate=pl.CostEstimate(flops=2 * 10**9, bytes_accessed=4 * 2**20, transcendentals=2 * 10**6),
    )(query_in, key_in, value_in, conv_weight, level_weights.reshape(5 * H, T), out_gain.reshape(1, H * DK))


def solution(mesh):
    return jax.shard_map(
        shards,
        mesh=mesh,
        in_specs=(
            P(("batch", "seq"), None),
            P(("batch", "seq"), None),
            P(("batch", "seq"), None),
            P(),
            P(None, None, ("batch", "seq")),
            P(),
        ),
        out_specs=P(("batch", "seq"), None),
        check_vma=False,
    )
```

time: 139 us -> 65.7 us (0.47)
  the two profiles are of different devices: /device:TPU:92 before, /device:TPU:2 now
where the time goes in v1:
time: 65.7 us; the launch traced here: 65.3 us
  Pallas kernels  58.3 us (89%)
  local copies, waits for them, and re-layouts  7.02 us (11%)
    pallas_call x1, Pallas kernels, shards(): pl.pallas_call(kernel, out_shape=jax.ShapeDtypeStruct((T, H * DK), BF16),...  58.3 us
    unnamed x13, local copies, waits for them, and re-layouts  7.02 us

profile of v1, /device:TPU:2, one launch (start us, length us, event | category | flops | bytes accessed | tf_op | source)
XLA Modules:
  0.0 65.3 jit_solution(9437876935886214152)
XLA Ops:
  0.0 0.0 copy-start
  0.0 1.2 %copy-done = bf16[512,1024]{1,0:T(8,128)(2,1)S(1)} copy-done((bf16[512,1024]{1,0:T(8,128)(2,1)S(1)}, bf16[512,1024]{1,0:T(8,128)(2,1)}, u32[]{:S(2)}) %copy-start) | copy-done | bytes 1048600
  1.2 0.0 copy-start.1
  1.2 1.2 %copy-done.1 = bf16[512,1024]{1,0:T(8,128)(2,1)S(1)} copy-done((bf16[512,1024]{1,0:T(8,128)(2,1)S(1)}, bf16[512,1024]{1,0:T(8,128)(2,1)}, u32[]{:S(2)}) %copy-start.1) | copy-done | bytes 1048600
  2.5 0.0 copy-start.2
  2.5 1.2 %copy-done.2 = bf16[512,1024]{1,0:T(8,128)(2,1)S(1)} copy-done((bf16[512,1024]{1,0:T(8,128)(2,1)S(1)}, bf16[512,1024]{1,0:T(8,128)(2,1)}, u32[]{:S(2)}) %copy-start.2) | copy-done | bytes 1048600
  3.7 0.0 copy-start.3
  3.7 0.9 %copy-done.3 = f32[5,8,512]{2,1,0:T(8,128)S(1)} copy-done((f32[5,8,512]{2,1,0:T(8,128)S(1)}, f32[5,8,512]{2,1,0:T(8,128)}, u32[]{:S(2)}) %copy-start.3) | copy-done | bytes 81944
  4.6 0.0 copy-start.4
  4.6 0.8 %copy-done.4 = f32[3,4,1024]{2,1,0:T(4,128)S(1)} copy-done((f32[3,4,1024]{2,1,0:T(4,128)S(1)}, f32[3,4,1024]{2,1,0:T(4,128)}, u32[]{:S(2)}) %copy-start.4) | copy-done | bytes 49176
  5.4 0.0 copy-start.5
  5.4 0.7 %copy-done.5 = f32[1024]{0:T(1024)S(1)} copy-done((f32[1024]{0:T(1024)S(1)}, f32[1024]{0:T(1024)}, u32[]{:S(2)}) %copy-start.5) | copy-done | bytes 4120
  6.0 58.3 %shard_map.64 = bf16[512,1024]{1,0:T(8,128)(2,1)S(1)} custom-call(bf16[512,1024]{1,0:T(8,128)(2,1)S(1)} %copy-done, bf16[512,1024]{1,0:T(8,128)(2,1)S(1)} %copy-done.1, bf16[512,1024]{1,0:T(8,128)(2,1)S(1)} %copy-done.2, f32[3,4,1024]{2,1,0:T(4,128)S(1)} %copy-done.4, f32[40,512]{1,0:T(8,128)S(1)} %bitcast.2, f32[1,1024]{1,0:T(1,128)S(1)} %bitcast.3), custom_call_target="tpu_custom_call" | custom-call | flops 2000000000 | bytes 4194304 | tf_op jit(solution)/shard_map/pallas_call | solution.py:375
  64.4 1.0 %copy.8 = bf16[512,1024]{1,0:T(8,128)(2,1)} copy(bf16[512,1024]{1,0:T(8,128)(2,1)S(1)} %shard_map.64) | data formatting | bytes 2097152
Async XLA Ops:
  0.0 1.2 %copy-start = (bf16[512,1024]{1,0:T(8,128)(2,1)S(1)}, bf16[512,1024]{1,0:T(8,128)(2,1)}, u32[]{:S(2)}) copy-start(bf16[512,1024]{1,0:T(8,128)(2,1)} %q_hbm.1) | copy-start | bytes 3145732
  1.2 1.2 %copy-start.1 = (bf16[512,1024]{1,0:T(8,128)(2,1)S(1)}, bf16[512,1024]{1,0:T(8,128)(2,1)}, u32[]{:S(2)}) copy-start(bf16[512,1024]{1,0:T(8,128)(2,1)} %k_hbm.1) | copy-start | bytes 3145732
  2.5 1.2 %copy-start.2 = (bf16[512,1024]{1,0:T(8,128)(2,1)S(1)}, bf16[512,1024]{1,0:T(8,128)(2,1)}, u32[]{:S(2)}) copy-start(bf16[512,1024]{1,0:T(8,128)(2,1)} %v_hbm.1) | copy-start | bytes 3145732
  3.7 0.9 %copy-start.3 = (f32[5,8,512]{2,1,0:T(8,128)S(1)}, f32[5,8,512]{2,1,0:T(8,128)}, u32[]{:S(2)}) copy-start(f32[5,8,512]{2,1,0:T(8,128)} %param.10) | copy-start | bytes 245764
  4.6 0.8 %copy-start.4 = (f32[3,4,1024]{2,1,0:T(4,128)S(1)}, f32[3,4,1024]{2,1,0:T(4,128)}, u32[]{:S(2)}) copy-start(f32[3,4,1024]{2,1,0:T(4,128)} %cw_ref.1) | copy-start | bytes 147460
  5.4 0.7 %copy-start.5 = (f32[1024]{0:T(1024)S(1)}, f32[1024]{0:T(1024)}, u32[]{:S(2)}) copy-start(f32[1024]{0:T(1024)} %param.11) | copy-start | bytes 12292

commit v2 on v1

--- a/solution.py
+++ b/solution.py
@@ -25,10 +25,11 @@
 
 
 def kernel(
-    q_hbm, k_hbm, v_hbm, cw_ref, lw_ref, gain_ref, out_hbm,
+    q_hbm, k_hbm, v_hbm, cw_hbm, lw_hbm, gain_hbm, out_hbm,
+    cw_ref, lw_ref, gain_ref,
     xin, tails, halo_f, halo_send, halo_recv, xf, xfs, qs, ks, vs, lwh, acc,
-    state, a_recv, b0_send, b1_send, yr, xt, buckets, obuf, own_f,
-    in_sem, tail_sem, out_sem, halo_sem, a_ss, a_rs, y_ss, y_rs, x_ss, x_rs, b_ss, b_rs,
+    state, a_recv, b0_send, b1_send, yr, xt, buckets, obuf, own_f, plane_f,
+    par_sem, in_sem, tail_sem, out_sem, halo_sem, a_ss, a_rs, y_ss, y_rs, x_ss, x_rs, b_ss, b_rs,
 ):
     me = lax.axis_index("seq")
     core = lax.axis_index("batch")
@@ -51,6 +52,12 @@
 
     for stream in range(3):
         tail(stream).start()
+    pars = [
+        pltpu.make_async_copy(src, dst, par_sem.at[i])
+        for i, (src, dst) in enumerate(((cw_hbm, cw_ref), (lw_hbm, lw_ref), (gain_hbm, gain_ref)))
+    ]
+    for copy in pars:
+        copy.start()
 
     def start_loads(step, carry):
         for stream in (1, 2):
@@ -86,15 +93,6 @@
         halo_send, halo_recv, halo_sem.at[0], halo_sem.at[1], device_id=(lax.rem(me + 1, 256), core), device_id_type=MESH
     )
 
-    pl.semaphore_wait(barrier, 18)
-    halo.start()
-
-    lw = jnp.concatenate([lw_ref[...], jnp.zeros((128 - 5 * H, T), F32)], axis=0).T
-    pos = lax.broadcasted_iota(jnp.int32, (T, 128), 0).astype(F32)
-    lane = lax.broadcasted_iota(jnp.int32, (T, 128), 1)
-    lw = jnp.where(lane < H, lw * lax.rsqrt(pos + 1.0), lw)
-    for head in range(H):
-        lwh[head] = lw if head == 0 else pltpu.roll(lw, 128 - head, 1)
 
     ones = jnp.ones((DK, DK), BF16)
 
@@ -138,7 +136,13 @@
             stream_head(stream, head, dst, None)
         return carry
 
-    lax.fori_loop(0, H, kv_step, 0)
+    for copy in pars:
+        copy.wait()
+    ahead = jnp.where(z < 4, H, 2)
+    lax.fori_loop(0, ahead, kv_step, 0)
+    pl.semaphore_wait(barrier, 18)
+    halo.start()
+    lax.fori_loop(ahead, H, kv_step, 0)
 
     halo.wait()
     halo_f[...] = jnp.where(me == 0, 0.0, halo_recv[...].astype(F32))
@@ -176,6 +180,13 @@
 
     lax.fori_loop(0, H - 1, state_step, 0)
     a_recv[z] = state_of(z).astype(BF16)
+
+    lw = jnp.concatenate([lw_ref[...], jnp.zeros((128 - 5 * H, T), F32)], axis=0).T
+    pos = lax.broadcasted_iota(jnp.int32, (T, 128), 0).astype(F32)
+    lane = lax.broadcasted_iota(jnp.int32, (T, 128), 1)
+    lw = jnp.where(lane < H, lw * lax.rsqrt(pos + 1.0), lw)
+    for head in range(H):
+        lwh[head] = lw if head == 0 else pltpu.roll(lw, 128 - head, 1)
 
     row_i = lax.broadcasted_iota(jnp.int32, (256, 256), 0)
     col_i = lax.broadcasted_iota(jnp.int32, (256, 256), 1)
@@ -201,104 +212,129 @@
         acc[head, pl.ds(256, 256), :] = w[256:] * o1
         return carry
 
-    lax.fori_loop(0, H, local_step, 0)
-
-    def wait_row(step, carry):
-        from_row(lax.rem(z + step, NZ)).wait_recv()
-        return carry
-
-    lax.fori_loop(1, NZ, wait_row, 0)
-    own_lo = None
-    row_sum = None
-    for zz in range(NZ):
-        s = a_recv[zz].astype(F32)
-        if zz % 4 == 0:
-            b0_send[zz] = jnp.zeros((DK, DK), BF16)
-            group = s
-        else:
-            b0_send[zz] = (group * ((1.0 / (T * (zz % 4))) ** 0.5)).astype(BF16)
-            group = group + s
-        if zz == 3:
-            own_lo = group
-        if zz == 7:
-            row_sum = own_lo + group
-    own_f[0] = own_lo
-    yr[y] = row_sum.astype(BF16)
-
-    def row_copy(src_y, dst_y, sem_y):
-        return pltpu.make_async_remote_copy(
-            yr.at[src_y], yr.at[src_y], y_ss.at[dst_y], y_rs.at[src_y], device_id=dev(x, dst_y, z), device_id_type=MESH
-        )
-
-    def send_rows(step, carry):
-        to = lax.rem(y + step, NY)
-        row_copy(y, to, y).start()
-        return carry
-
-    lax.fori_loop(1, NY, send_rows, 0)
+    def from_group(first):
+        def wait(source, carry):
+            @pl.when(source != z)
+            def _():
+                from_row(source).wait_recv()
+
+            return carry
+
+        lax.fori_loop(first, first + 4, wait, 0)
+
+    def group_sum(first):
+        group = a_recv[first].astype(F32)
+        for digit in range(1, 4):
+            b0_send[first + digit] = (group * ((1.0 / (T * digit)) ** 0.5)).astype(BF16)
+            group = group + a_recv[first + digit].astype(F32)
+        return group
+
+    odd = lax.rem(y, 2)
+    pair = y // 2
+
+    def needs(level, zz):
+        return (lax.rem(zz, 4) != 0, (zz >= 4) | (odd == 1), pair > 0, x > 0)[level]
 
     def bucket_copy(level, src, to, head):
         return pltpu.make_async_remote_copy(
             src, buckets.at[level, head], b_ss.at[level, to], b_rs.at[level, head], device_id=dev(x, y, to), device_id_type=MESH
         )
 
-    def send_b0(step, carry):
-        to = lax.rem(z + step, NZ)
-        bucket_copy(0, b0_send.at[to], to, z).start()
-        return carry
-
-    lax.fori_loop(1, NZ, send_b0, 0)
-    buckets[0, z] = b0_send[z]
+    def sent(level, to):
+        if level == 0:
+            return b0_send.at[to]
+        return b1_send.at[to // 4 if level == 1 else level]
+
+    def send_bucket(level, first):
+        def step(to, carry):
+            @pl.when((to != z) & needs(level, to))
+            def _():
+                bucket_copy(level, sent(level, to), to, z).start()
+
+            return carry
+
+        lax.fori_loop(first, first + 4, step, 0)
+
+    def row_copy(src_y, dst_y):
+        return pltpu.make_async_remote_copy(
+            yr.at[src_y], yr.at[src_y], y_ss.at[dst_y], y_rs.at[src_y], device_id=dev(x, dst_y, z), device_id_type=MESH
+        )
+
+    def plane_copy(src_x, dst_x):
+        return pltpu.make_async_remote_copy(
+            xt.at[src_x], xt.at[src_x], x_ss.at[dst_x], x_rs.at[src_x], device_id=dev(dst_x, y, z), device_id_type=MESH
+        )
+
+    lax.fori_loop(0, 4, local_step, 0)
+    from_group(0)
+    own_f[0] = group_sum(0)
+    send_bucket(0, 0)
+    lax.fori_loop(4, H, local_step, 0)
+
+    from_group(4)
+    yr[y] = (own_f[0] + group_sum(4)).astype(BF16)
+
+    def send_rows(step, carry):
+        row_copy(y, lax.rem(y + step, NY)).start()
+        return carry
+
+    lax.fori_loop(1, NY, send_rows, 0)
+
+    @pl.when(needs(0, z))
+    def _():
+        buckets[0, z] = b0_send[z]
+
 
     def wait_rows(step, carry):
-        src = lax.rem(y + step, NY)
-        row_copy(src, src, src).wait_recv()
-        return carry
-
-    lax.fori_loop(1, NY, wait_rows, 0)
-
-    odd = lax.rem(y, 2)
-    pair = y // 2
+        src = lax.rem(y + NY - step, NY)
+        row_copy(src, src).wait_recv()
+        return carry
+
+    wait_rows(1, 0)
     before = jnp.where(odd == 1, 1.0, 0.0) * yr[jnp.maximum(y - 1, 0)].astype(F32)
     b1_send[0] = (level_factor(2 * odd, 1) * before).astype(BF16)
     b1_send[1] = (level_factor(2 * odd + 1, 1) * (before + own_f[0])).astype(BF16)
+    send_bucket(1, 0)
+    send_bucket(0, 4)
+    buckets[1, z] = b1_send[z // 4]
+
+    lax.fori_loop(2, NY, wait_rows, 0)
     earlier = jnp.zeros((DK, DK), F32)
     plane = jnp.zeros((DK, DK), F32)
     for yy in range(NY):
         r = yr[yy].astype(F32)
         plane = plane + r
         earlier = earlier + jnp.where(yy < 2 * pair, 1.0, 0.0) * r
+    xt[x] = plane.astype(BF16)
+    for xx in range(1, NX):
+
+        @pl.when(xx > x)
+        def _():
+            plane_copy(x, xx).start()
+
     b1_send[2] = (level_factor(pair, 2) * earlier).astype(BF16)
-    xt[x] = plane.astype(BF16)
-
-    def plane_copy(src_x, dst_x):
-        return pltpu.make_async_remote_copy(
-            xt.at[src_x], xt.at[src_x], x_ss.at[dst_x], x_rs.at[src_x], device_id=dev(dst_x, y, z), device_id_type=MESH
-        )
-
-    for step in range(1, NX):
-        plane_copy(x, lax.rem(x + step, NX)).start()
-
-    def send_b12(step, carry):
-        to = lax.rem(z + step, NZ)
-        bucket_copy(1, b1_send.at[to // 4], to, z).start()
-        return carry
-
-    lax.fori_loop(1, NZ, send_b12, 0)
-
-    def send_b2(step, carry):
-        to = lax.rem(z + step, NZ)
-        bucket_copy(2, b1_send.at[2], to, z).start()
-        return carry
-
-    lax.fori_loop(1, NZ, send_b2, 0)
-    buckets[1, z] = b1_send[z // 4]
+    send_bucket(2, 0)
+    send_bucket(1, 4)
     buckets[2, z] = b1_send[2]
+
+    plane_f[...] = jnp.zeros((DK, DK), F32)
+    for xx in range(NX - 1):
+
+        @pl.when(xx < x)
+        def _():
+            plane_copy(xx, xx).wait_recv()
+            plane_f[...] += xt[xx].astype(F32)
+
+    b1_send[3] = (level_factor(x, 3) * plane_f[...]).astype(BF16)
+    send_bucket(3, 0)
+    send_bucket(2, 4)
+    send_bucket(3, 4)
+    buckets[3, z] = b1_send[3]
 
     def wait_bucket(level, head):
         @pl.when(head != z)
         def _():
-            bucket_copy(level, b1_send.at[2], head, head).wait_recv()
+            bucket_copy(level, b1_send.at[3], head, head).wait_recv()
 
     def project(level, head):
         return weight(head, level + 1) * jnp.dot(qs[head], buckets[level, head], preferred_element_type=F32)
@@ -310,23 +346,9 @@
             acc[head] += project(level, head)
             return carry
 
-        lax.fori_loop(0, H, step, 0)
-
-    for step in range(1, NX):
-        src = lax.rem(x + step, NX)
-        plane_copy(src, src).wait_recv()
-    earlier = jnp.zeros((DK, DK), F32)
-    for xx in range(NX):
-        earlier = earlier + jnp.where(xx < x, 1.0, 0.0) * xt[xx].astype(F32)
-    b1_send[3] = (level_factor(x, 3) * earlier).astype(BF16)
-
-    def send_b3(step, carry):
-        to = lax.rem(z + step, NZ)
-        bucket_copy(3, b1_send.at[3], to, z).start()
-        return carry
-
-    lax.fori_loop(1, NZ, send_b3, 0)
-    buckets[3, z] = b1_send[3]
+        @pl.when(needs(level, z))
+        def _():
+            lax.fori_loop(0, H, step, 0)
 
     add_level(0)
     add_level(1)
@@ -338,7 +360,11 @@
 
     def last_step(i, carry):
         head = lax.rem(z + i, NZ)
-        wait_bucket(3, head)
+
+        @pl.when(x > 0)
+        def _():
+            wait_bucket(3, head)
+
         mixed = acc[head] + project(3, head)
         total = jnp.dot((mixed * mixed).astype(BF16), ones, preferred_element_type=F32)
         cols = pl.ds(pl.multiple_of(head * DK, DK), DK)
@@ -346,20 +372,31 @@
         store(head).start()
         return carry
 
+    @pl.when(x == 0)
+    def _():
+        for head in range(H):
+            buckets[3, head] = jnp.zeros((DK, DK), BF16)
+
     lax.fori_loop(0, H, last_step, 0)
 
     def drain(step, carry):
         to = lax.rem(z + step, NZ)
         from_row(to).wait_send()
-        ty = lax.rem(y + step, NY)
-        row_copy(y, ty, y).wait_send()
+        row_copy(y, lax.rem(y + step, NY)).wait_send()
         for level in range(4):
-            bucket_copy(level, b1_send.at[2], to, z).wait_send()
+
+            @pl.when(needs(level, to))
+            def _():
+                bucket_copy(level, b1_send.at[3], to, z).wait_send()
+
         return carry
 
     lax.fori_loop(1, NZ, drain, 0)
-    for step in range(1, NX):
-        plane_copy(x, lax.rem(x + step, NX)).wait_send()
+    for xx in range(1, NX):
+
+        @pl.when(xx > x)
+        def _():
+            plane_copy(x, xx).wait_send()
 
     def stored(head, carry):
         store(head).wait()
@@ -369,15 +406,17 @@
 
 
 def shards(query_in, key_in, value_in, conv_weight, level_weights, out_gain):
-    anywhere = pl.BlockSpec(memory_space=pl.ANY)
-    vmem = pl.BlockSpec(memory_space=pltpu.VMEM)
+    hbm = pl.BlockSpec(memory_space=pltpu.HBM)
     dma = pltpu.SemaphoreType.DMA
     return pl.pallas_call(
         kernel,
         out_shape=jax.ShapeDtypeStruct((T, H * DK), BF16),
-        in_specs=[anywhere] * 3 + [vmem] * 3,
-        out_specs=anywhere,
+        in_specs=[hbm] * 6,
+        out_specs=hbm,
         scratch_shapes=[
+            pltpu.VMEM((3, 4, H * DK), F32),
+            pltpu.VMEM((5 * H, T), F32),
+            pltpu.VMEM((1, H * DK), F32),
             pltpu.VMEM((3, H, T, DK), BF16),
             pltpu.VMEM((3, 16, H * DK), BF16),
             pltpu.VMEM((16, H * DK), F32),
@@ -399,6 +438,8 @@
             pltpu.VMEM((4, H, DK, DK), BF16),
             pltpu.VMEM((H, T, DK), BF16),
             pltpu.VMEM((1, DK, DK), F32),
+            pltpu.VMEM((DK, DK), F32),
+            dma((3,)),
             dma((3, H)),
             dma((3,)),
             dma((H,)),
@@ -413,7 +454,7 @@
             dma((4, NZ)),
         ],
         compiler_params=pltpu.CompilerParams(
-            collective_id=0, has_side_effects=True, vmem_limit_bytes=48 * 1024 * 1024
+            collective_id=0, has_side_effects=True, vmem_limit_bytes=60 * 1024 * 1024
         ),
         cost_estimate=pl.CostEstimate(flops=2 * 10**9, bytes_accessed=4 * 2**20, transcendentals=2 * 10**6),
     )(query_in, key_in, value_in, conv_weight, level_weights.reshape(5 * H, T), out_gain.reshape(1, H * DK))

time: 65.7 us -> 54 us (0.82)
  the two profiles are of different devices: /device:TPU:2 before, /device:TPU:30 now
where the time goes in v2:
time: 54 us; the launch traced here: 53.9 us
  Pallas kernels  51.6 us (96%)
  local copies, waits for them, and re-layouts  2.26 us (4%)
    pallas_call x1, Pallas kernels, shards(): pl.pallas_call(kernel, out_shape=jax.ShapeDtypeStruct((T, H * DK), BF16),...  51.6 us
    unnamed x1, local copies, waits for them, and re-layouts  2.26 us

profile of v2, /device:TPU:30, one launch (start us, length us, event | category | flops | bytes accessed | tf_op | source)
XLA Modules:
  0.0 53.9 jit_solution(6552273639572654049)
XLA Ops:
  0.0 51.6 %shard_map.64 = bf16[512,1024]{1,0:T(8,128)(2,1)} custom-call(bf16[512,1024]{1,0:T(8,128)(2,1)} %q_hbm.1, bf16[512,1024]{1,0:T(8,128)(2,1)} %k_hbm.1, bf16[512,1024]{1,0:T(8,128)(2,1)} %v_hbm.1, f32[3,4,1024]{2,1,0:T(4,128)} %cw_hbm.1, f32[40,512]{1,0:T(8,128)} %bitcast.2, f32[1,1024]{1,0:T(1,128)} %bitcast.3), custom_call_target="tpu_custom_call" | custom-call | flops 2000000000 | bytes 4194304 | tf_op jit(solution)/shard_map/pallas_call | solution.py:411
  51.6 2.3 %copy.8 = bf16[512,1024]{1,0:T(8,128)(2,1)} copy(bf16[512,1024]{1,0:T(8,128)(2,1)} %shard_map.64) | data formatting | bytes 2097152

commit v3 on v2

--- a/solution.py
+++ b/solution.py
@@ -94,8 +94,6 @@
     )
 
 
-    ones = jnp.ones((DK, DK), BF16)
-
     def taps(stream, head):
         cols = pl.ds(pl.multiple_of(head * DK, DK), DK)
         return [cw_ref[stream, pl.ds(j, 1), cols] for j in range(4)]
@@ -104,8 +102,7 @@
         return c * pl.reciprocal(1.0 + jnp.exp(-c), approx=True)
 
     def unit(a):
-        total = jnp.dot((a * a).astype(BF16), ones, preferred_element_type=F32)
-        return a * lax.rsqrt(total + EPS)
+        return a * lax.rsqrt(jnp.sum(a * a, axis=-1, keepdims=True) + EPS)
 
     def conv_rows(src, w, row, count):
         c = w[0] * src[pl.ds(row + 5, count), :]
@@ -162,14 +159,19 @@
             device_id=dev(x, y, source), device_id_type=MESH,
         )
 
-    def state_of(head):
-        for stream, dst in ((1, ks), (2, vs)):
-            xfs[pl.ds(5, 3), :] = halo_rows(stream, head)
-            xfs[pl.ds(8, 16), :] = xin[stream, head, pl.ds(0, 16), :].astype(F32)
-            a = conv_rows(xfs, taps(stream, head), 0, 16)
+    for stream, dst in ((1, ks), (2, vs)):
+        for head in range(H):
+            cols = slice(head * DK, (head + 1) * DK)
+            xfs[stream - 1, head, pl.ds(5, 3), :] = halo_f[3 * stream : 3 * stream + 3, cols]
+            xfs[stream - 1, head, pl.ds(8, 16), :] = xin[stream, head, pl.ds(0, 16), :].astype(F32)
+    for stream, dst in ((1, ks), (2, vs)):
+        for head in range(H):
+            a = conv_rows(xfs.at[stream - 1, head], taps(stream, head), 0, 16)
             if stream == 1:
                 a = unit(a)
             dst[head, pl.ds(0, 16), :] = a.astype(BF16)
+
+    def state_of(head):
         return lax.dot_general(ks[head], vs[head], (((0,), (0,)), ((), ())), preferred_element_type=F32)
 
     def state_step(step, carry):
@@ -265,11 +267,11 @@
             xt.at[src_x], xt.at[src_x], x_ss.at[dst_x], x_rs.at[src_x], device_id=dev(dst_x, y, z), device_id_type=MESH
         )
 
-    lax.fori_loop(0, 4, local_step, 0)
+    lax.fori_loop(0, 3, local_step, 0)
     from_group(0)
     own_f[0] = group_sum(0)
     send_bucket(0, 0)
-    lax.fori_loop(4, H, local_step, 0)
+    lax.fori_loop(3, 6, local_step, 0)
 
     from_group(4)
     yr[y] = (own_f[0] + group_sum(4)).astype(BF16)
@@ -290,6 +292,7 @@
         row_copy(src, src).wait_recv()
         return carry
 
+    lax.fori_loop(6, H, local_step, 0)
     wait_rows(1, 0)
     before = jnp.where(odd == 1, 1.0, 0.0) * yr[jnp.maximum(y - 1, 0)].astype(F32)
     b1_send[0] = (level_factor(2 * odd, 1) * before).astype(BF16)
@@ -339,45 +342,46 @@
     def project(level, head):
         return weight(head, level + 1) * jnp.dot(qs[head], buckets[level, head], preferred_element_type=F32)
 
+    def wait_level(level, first):
+        def step(head, carry):
+            wait_bucket(level, head)
+            return carry
+
+        @pl.when(needs(level, z))
+        def _():
+            lax.fori_loop(first, first + 4, step, 0)
+
     def add_level(level):
-        def step(i, carry):
-            head = lax.rem(z + i, NZ)
-            wait_bucket(level, head)
-            acc[head] += project(level, head)
-            return carry
-
         @pl.when(needs(level, z))
         def _():
-            lax.fori_loop(0, H, step, 0)
-
+            for first in (0, 4):
+                wait_level(level, first)
+                for head in range(first, first + 4):
+                    acc[head] += project(level, head)
+
+    def store(head):
+        cols = pl.ds(head * DK, DK)
+        return pltpu.make_async_copy(obuf.at[head], out_hbm.at[:, cols], out_sem.at[head])
+
+    def clear(level):
+        @pl.when(jnp.logical_not(needs(level, z)))
+        def _():
+            for head in range(H):
+                buckets[level, head] = jnp.zeros((DK, DK), BF16)
+
+    clear(2)
+    clear(3)
     add_level(0)
     add_level(1)
-    add_level(2)
-
-    def store(head):
-        cols = pl.ds(pl.multiple_of(head * DK, DK), DK)
-        return pltpu.make_async_copy(obuf.at[head], out_hbm.at[:, cols], out_sem.at[head])
-
-    def last_step(i, carry):
-        head = lax.rem(z + i, NZ)
-
-        @pl.when(x > 0)
-        def _():
-            wait_bucket(3, head)
-
-        mixed = acc[head] + project(3, head)
-        total = jnp.dot((mixed * mixed).astype(BF16), ones, preferred_element_type=F32)
-        cols = pl.ds(pl.multiple_of(head * DK, DK), DK)
-        obuf[head] = (mixed * lax.rsqrt(total * (1.0 / DK) + EPS) * gain_ref[:, cols]).astype(BF16)
-        store(head).start()
-        return carry
-
-    @pl.when(x == 0)
-    def _():
-        for head in range(H):
-            buckets[3, head] = jnp.zeros((DK, DK), BF16)
-
-    lax.fori_loop(0, H, last_step, 0)
+    for first in (0, 4):
+        wait_level(2, first)
+        wait_level(3, first)
+        for head in range(first, first + 4):
+            mixed = acc[head] + project(2, head) + project(3, head)
+            mean = jnp.sum(mixed * mixed, axis=-1, keepdims=True) * (1.0 / DK)
+            gain = gain_ref[:, head * DK : (head + 1) * DK]
+            obuf[head] = (mixed * lax.rsqrt(mean + EPS) * gain).astype(BF16)
+            store(head).start()
 
     def drain(step, carry):
         to = lax.rem(z + step, NZ)
@@ -398,11 +402,8 @@
         def _():
             plane_copy(x, xx).wait_send()
 
-    def stored(head, carry):
+    for head in range(H):
         store(head).wait()
-        return carry
-
-    lax.fori_loop(0, H, stored, 0)
 
 
 def shards(query_in, key_in, value_in, conv_weight, level_weights, out_gain):
@@ -423,7 +424,7 @@
             pltpu.VMEM((16, H * DK), BF16),
             pltpu.VMEM((16, H * DK), BF16),
             pltpu.VMEM((3, T + 8, DK), F32),
-            pltpu.VMEM((24, DK), F32),
+            pltpu.VMEM((2, H, 24, DK), F32),
             pltpu.VMEM((H, T, DK), BF16),
             pltpu.VMEM((H, T, DK), BF16),
             pltpu.VMEM((H, T, DK), BF16),

time: 54 us -> 52.5 us (0.972)
  the two profiles are of different devices: /device:TPU:30 before, /device:TPU:4 now
where the time goes in v3:
time: 52.5 us; the launch traced here: 52.3 us
  Pallas kernels  50 us (95%)
  local copies, waits for them, and re-layouts  2.26 us (4%)
    pallas_call x1, Pallas kernels, shards(): pl.pallas_call(kernel, out_shape=jax.ShapeDtypeStruct((T, H * DK), BF16),...  50 us
    unnamed x1, local copies, waits for them, and re-layouts  2.26 us

profile of v3, /device:TPU:4, one launch (start us, length us, event | category | flops | bytes accessed | tf_op | source)
XLA Modules:
  0.0 52.3 jit_solution(13690941396200987846)
XLA Ops:
  0.0 50.0 %shard_map.64 = bf16[512,1024]{1,0:T(8,128)(2,1)} custom-call(bf16[512,1024]{1,0:T(8,128)(2,1)} %q_hbm.1, bf16[512,1024]{1,0:T(8,128)(2,1)} %k_hbm.1, bf16[512,1024]{1,0:T(8,128)(2,1)} %v_hbm.1, f32[3,4,1024]{2,1,0:T(4,128)} %cw_hbm.1, f32[40,512]{1,0:T(8,128)} %bitcast.2, f32[1,1024]{1,0:T(1,128)} %bitcast.3), custom_call_target="tpu_custom_call" | custom-call | flops 2000000000 | bytes 4194304 | tf_op jit(solution)/shard_map/pallas_call | solution.py:412
  50.0 2.3 %copy.8 = bf16[512,1024]{1,0:T(8,128)(2,1)} copy(bf16[512,1024]{1,0:T(8,128)(2,1)} %shard_map.64) | data formatting | bytes 2097152

commit v4 on v3

--- a/solution.py
+++ b/solution.py
@@ -135,7 +135,7 @@
 
     for copy in pars:
         copy.wait()
-    ahead = jnp.where(z < 4, H, 2)
+    ahead = jnp.where(z < 4, 4, 1)
     lax.fori_loop(0, ahead, kv_step, 0)
     pl.semaphore_wait(barrier, 18)
     halo.start()
@@ -292,13 +292,14 @@
         row_copy(src, src).wait_recv()
         return carry
 
+    send_bucket(0, 4)
     lax.fori_loop(6, H, local_step, 0)
     wait_rows(1, 0)
     before = jnp.where(odd == 1, 1.0, 0.0) * yr[jnp.maximum(y - 1, 0)].astype(F32)
     b1_send[0] = (level_factor(2 * odd, 1) * before).astype(BF16)
     b1_send[1] = (level_factor(2 * odd + 1, 1) * (before + own_f[0])).astype(BF16)
     send_bucket(1, 0)
-    send_bucket(0, 4)
+    send_bucket(1, 4)
     buckets[1, z] = b1_send[z // 4]
 
     lax.fori_loop(2, NY, wait_rows, 0)
@@ -317,7 +318,6 @@
 
     b1_send[2] = (level_factor(pair, 2) * earlier).astype(BF16)
     send_bucket(2, 0)
-    send_bucket(1, 4)
     buckets[2, z] = b1_send[2]
 
     plane_f[...] = jnp.zeros((DK, DK), F32)

time: 52.5 us -> 50.4 us (0.960)
  the two profiles are of different devices: /device:TPU:4 before, /device:TPU:20 now
where the time goes in v4:
time: 50.4 us; the launch traced here: 50.2 us
  Pallas kernels  48 us (95%)
  local copies, waits for them, and re-layouts  2.26 us (4%)
    pallas_call x1, Pallas kernels, shards(): pl.pallas_call(kernel, out_shape=jax.ShapeDtypeStruct((T, H * DK), BF16),...  48 us
    unnamed x1, local copies, waits for them, and re-layouts  2.26 us

profile of v4, /device:TPU:20, one launch (start us, length us, event | category | flops | bytes accessed | tf_op | source)
XLA Modules:
  0.0 50.2 jit_solution(16539648930855329203)
XLA Ops:
  0.0 48.0 %shard_map.64 = bf16[512,1024]{1,0:T(8,128)(2,1)} custom-call(bf16[512,1024]{1,0:T(8,128)(2,1)} %q_hbm.1, bf16[512,1024]{1,0:T(8,128)(2,1)} %k_hbm.1, bf16[512,1024]{1,0:T(8,128)(2,1)} %v_hbm.1, f32[3,4,1024]{2,1,0:T(4,128)} %cw_hbm.1, f32[40,512]{1,0:T(8,128)} %bitcast.2, f32[1,1024]{1,0:T(1,128)} %bitcast.3), custom_call_target="tpu_custom_call" | custom-call | flops 2000000000 | bytes 4194304 | tf_op jit(solution)/shard_map/pallas_call | solution.py:412
  48.0 2.3 %copy.8 = bf16[512,1024]{1,0:T(8,128)(2,1)} copy(bf16[512,1024]{1,0:T(8,128)(2,1)} %shard_map.64) | data formatting | bytes 2097152

commit v5 on v4

--- a/solution.py
+++ b/solution.py
@@ -276,11 +276,8 @@
     from_group(4)
     yr[y] = (own_f[0] + group_sum(4)).astype(BF16)
 
-    def send_rows(step, carry):
+    for step in (1, 4, 5, 3, 6, 2, 7):
         row_copy(y, lax.rem(y + step, NY)).start()
-        return carry
-
-    lax.fori_loop(1, NY, send_rows, 0)
 
     @pl.when(needs(0, z))
     def _():

time: 50.4 us -> 50.1 us (level)
  the two profiles are of different devices: /device:TPU:20 before, /device:TPU:94 now
where the time goes in v5:
time: 50.1 us; the launch traced here: 49.9 us
  Pallas kernels  47.7 us (95%)
  local copies, waits for them, and re-layouts  2.26 us (5%)
    pallas_call x1, Pallas kernels, shards(): pl.pallas_call(kernel, out_shape=jax.ShapeDtypeStruct((T, H * DK), BF16),...  47.7 us
    unnamed x1, local copies, waits for them, and re-layouts  2.26 us

profile of v5, /device:TPU:94, one launch (start us, length us, event | category | flops | bytes accessed | tf_op | source)
XLA Modules:
  0.0 49.9 jit_solution(2580270917175508949)
XLA Ops:
  0.0 47.7 %shard_map.64 = bf16[512,1024]{1,0:T(8,128)(2,1)} custom-call(bf16[512,1024]{1,0:T(8,128)(2,1)} %q_hbm.1, bf16[512,1024]{1,0:T(8,128)(2,1)} %k_hbm.1, bf16[512,1024]{1,0:T(8,128)(2,1)} %v_hbm.1, f32[3,4,1024]{2,1,0:T(4,128)} %cw_hbm.1, f32[40,512]{1,0:T(8,128)} %bitcast.2, f32[1,1024]{1,0:T(1,128)} %bitcast.3), custom_call_target="tpu_custom_call" | custom-call | flops 2000000000 | bytes 4194304 | tf_op jit(solution)/shard_map/pallas_call | solution.py:409
  47.7 2.3 %copy.8 = bf16[512,1024]{1,0:T(8,128)(2,1)} copy(bf16[512,1024]{1,0:T(8,128)(2,1)} %shard_map.64) | data formatting | bytes 2097152
